TPU v7x, 32 devices: a whole 2x2x4 slice. The times are simulated.
32 devices in a mesh: gx: 4 (over z), gy: 8 (over y, x, core).
Axes of the slice: x: 2, y: 2, z: 4, core: 2. Of those that a mesh axis runs over, the one named last changes fastest.
Arguments:
- image: float32 [64, 256, 256], P('gx', 'gy'), may hold values from -6 to 6
- phases: int32 [64, 256, 256], P('gx', 'gy'), may hold values from 0 to 2
- phase_table: float32 [2, 3], replicated, may hold values from 0.2 to 8
- start_potential: float32 [64, 256, 256], P('gx', 'gy'), may hold values from 0 to 1
Outputs:
- conductivity: float32 [64, 256, 256], P('gx', 'gy')
- potential: float32 [64, 256, 256], P('gx', 'gy')
Inputs may be any that keep to these rules, and one draw needn't show every extreme that they name: `phases`: 0 fibre, 1 binder, 2 pore.
All inputs are finite; a program needn't handle non-finite values.
Results may differ from a plain program's by a relative error of at most 0.00005.
Values sent between devices are 32-bit elements; how exact they have to be, the bound alone decides.
A program may use at most 128 MiB of HBM per device.

v0:
```python
import functools
import math

import jax
import jax.numpy as jnp
import ml_dtypes
import numpy as np
from jax import lax
from jax.experimental import pallas as pl
from jax.experimental.pallas import tpu as pltpu
from jax.sharding import PartitionSpec as P

SWEEPS = 3
PHASES = 3
DERIV = 3
SMOOTH = 12
IMG_X = DERIV + SMOOTH
IMG_Y = 16
POT_X = SWEEPS
POT_Y = 8
MESH = pl.DeviceIdType.MESH
F32 = jnp.float32
BF16 = jnp.bfloat16


def gauss_taps(sigma, reach, order):
    values = [math.exp(-t * t / (2.0 * sigma * sigma)) for t in range(-reach, reach + 1)]
    total = sum(values)
    values = [value / total for value in values]
    if order == 1:
        values = [(i - reach) * values[i] / (sigma * sigma) for i in range(2 * reach + 1)]
    return values


NEAR = gauss_taps(1.0, DERIV, 0)
SLOPE = gauss_taps(1.0, DERIV, 1)
WIDE = gauss_taps(4.0, SMOOTH, 0)


def halves(matrix):
    high = matrix.astype(ml_dtypes.bfloat16)
    low = (matrix - high.astype(np.float32)).astype(ml_dtypes.bfloat16)
    return high, low


def band(out_len, in_len, margin, taps, first=0, last=None):
    reach = (len(taps) - 1) // 2
    matrix = np.zeros((out_len, in_len), np.float32)
    for i in range(first, out_len if last is None else last):
        for t in range(-reach, reach + 1):
            k = i + margin + t
            if 0 <= k < in_len:
                matrix[i, k] = taps[t + reach]
    return matrix


def left_weights(matrix):
    high, low = halves(matrix)
    return np.concatenate([high, high, low], axis=1)


def right_weights(*matrices):
    parts = []
    for matrix in matrices:
        parts += list(halves(np.ascontiguousarray(matrix.T)))
    return np.concatenate(parts, axis=1)


def neighbours():
    gx, gy = lax.axis_index("gx"), lax.axis_index("gy")
    nx, ny = lax.axis_size("gx"), lax.axis_size("gy")
    has_x = (gx > 0, gx < nx - 1)
    has_y = (gy > 0, gy < ny - 1)
    at_x = ((gx - 1, gy), (gx + 1, gy))
    at_y = ((gx, gy - 1), (gx, gy + 1))
    return has_x, has_y, at_x, at_y


def greet():
    has_x, has_y, at_x, at_y = neighbours()
    barrier = pltpu.get_barrier_semaphore()
    for has, at in zip(has_x + has_y, at_x + at_y):
        @pl.when(has)
        def _(at=at):
            pl.semaphore_signal(barrier, inc=1, device_id=at, device_id_type=MESH)
    pl.semaphore_wait(barrier, sum(has.astype(jnp.int32) for has in has_x + has_y))


class Exchange:
    def __init__(self, own, ext, hx, hy, cuts, send, recv, local):
        self.own, self.ext, self.hx, self.hy, self.cuts = own, ext, hx, hy, cuts
        self.send, self.recv, self.local = send, recv, local
        self.nx, self.ny = own.shape[0], own.shape[1]
        self.has_x, self.has_y, self.at_x, self.at_y = neighbours()

    @staticmethod
    def count(cuts):
        return 2 + 6 * len(cuts)

    def remote(self, src, dst, index, at):
        return pltpu.make_async_remote_copy(
            src_ref=src, dst_ref=dst, send_sem=self.send.at[index],
            recv_sem=self.recv.at[index], device_id=at, device_id_type=MESH)

    def halo_rows(self, d, cut):
        a, b = cut
        if d == 0:
            return self.nx + self.hx + a, b - a
        return self.hx - b, b - a

    def copy_x(self, d, c):
        a, b = self.cuts[c]
        row, size = self.halo_rows(d, (a, b))
        start = a if d == 0 else self.nx - b
        return self.remote(
            self.own.at[pl.ds(start, size)],
            self.ext.at[pl.ds(row, size), pl.ds(self.hy, self.ny)],
            2 + d * len(self.cuts) + c, self.at_x[d])

    def copy_y(self, d):
        src = 0 if d == 0 else self.ny - self.hy
        dst = self.hy + self.ny if d == 0 else 0
        return self.remote(
            self.own.at[:, pl.ds(src, self.hy)],
            self.ext.at[pl.ds(self.hx, self.nx), pl.ds(dst, self.hy)],
            d, self.at_y[d])

    def copy_corner(self, side, d, c):
        row, size = self.halo_rows(side, self.cuts[c])
        src = self.hy if d == 0 else self.ny
        dst = self.hy + self.ny if d == 0 else 0
        n = len(self.cuts)
        return self.remote(
            self.ext.at[pl.ds(row, size), pl.ds(src, self.hy)],
            self.ext.at[pl.ds(row, size), pl.ds(dst, self.hy)],
            2 + 2 * n + (side * 2 + d) * n + c, self.at_y[d])

    def copy_own(self):
        return pltpu.make_async_copy(
            self.own, self.ext.at[pl.ds(self.hx, self.nx), pl.ds(self.hy, self.ny)], self.local)

    def start(self):
        for c in range(len(self.cuts)):
            for d in range(2):
                pl.when(self.has_x[d])(lambda d=d, c=c: self.copy_x(d, c).start())
        for d in range(2):
            pl.when(self.has_y[d])(lambda d=d: self.copy_y(d).start())
        self.copy_own().start()
        rows, cols, z = self.ext.shape
        for d in range(2):
            @pl.when(jnp.logical_not(self.has_x[d]))
            def _(d=d):
                at = 0 if d == 0 else self.hx + self.nx
                self.ext[pl.ds(at, self.hx)] = jnp.zeros((self.hx, cols, z), F32)

            @pl.when(jnp.logical_not(self.has_y[d]))
            def _(d=d):
                at = 0 if d == 0 else self.hy + self.ny
                self.ext[:, pl.ds(at, self.hy)] = jnp.zeros((rows, self.hy, z), F32)

    def forward(self):
        for c in range(len(self.cuts)):
            for side in range(2):
                @pl.when(self.has_x[1 - side])
                def _(side=side, c=c):
                    self.copy_x(side, c).wait_recv()
                    for d in range(2):
                        pl.when(self.has_y[d])(
                            lambda d=d: self.copy_corner(side, d, c).start())

    def finish(self):
        self.copy_own().wait()
        for d in range(2):
            pl.when(self.has_y[1 - d])(lambda d=d: self.copy_y(d).wait_recv())
            for c in range(len(self.cuts)):
                for side in range(2):
                    pl.when(jnp.logical_and(self.has_x[1 - side], self.has_y[1 - d]))(
                        lambda d=d, c=c, side=side: self.copy_corner(side, d, c).wait_recv())
        for d in range(2):
            pl.when(self.has_y[d])(lambda d=d: self.copy_y(d).wait_send())
            for c in range(len(self.cuts)):
                pl.when(self.has_x[d])(lambda d=d, c=c: self.copy_x(d, c).wait_send())
                for side in range(2):
                    pl.when(jnp.logical_and(self.has_x[1 - side], self.has_y[d]))(
                        lambda d=d, c=c, side=side: self.copy_corner(side, d, c).wait_send())


def exchange_kernel(plans, *refs):
    n = len(plans)
    owns, exts, sems = refs[:n], refs[n:2 * n], refs[2 * n:]
    greet()
    parts = [
        Exchange(own, ext, *plan, *sems[3 * i:3 * i + 3])
        for i, (own, ext, plan) in enumerate(zip(owns, exts, plans))
    ]
    for part in parts:
        part.start()
    for part in parts:
        part.forward()
    for part in parts:
        part.finish()


def exchange(arrays, plans, collective_id):
    shapes, scratch = [], []
    for array, (hx, hy, cuts) in zip(arrays, plans):
        x, y, z = array.shape
        shapes.append(jax.ShapeDtypeStruct((x + 2 * hx, y + 2 * hy, z), F32))
        count = Exchange.count(cuts)
        scratch += [pltpu.SemaphoreType.DMA((count,))] * 2 + [pltpu.SemaphoreType.DMA]
    return pl.pallas_call(
        functools.partial(exchange_kernel, plans),
        out_shape=shapes,
        in_specs=[pl.BlockSpec(memory_space=pl.ANY)] * len(arrays),
        out_specs=[pl.BlockSpec(memory_space=pltpu.VMEM)] * len(arrays),
        scratch_shapes=scratch,
        compiler_params=pltpu.CompilerParams(
            collective_id=collective_id, has_side_effects=True,
            vmem_limit_bytes=32 * 1024 * 1024),
    )(*arrays)


def split(value):
    high = value.astype(BF16)
    return high, (value - high.astype(F32)).astype(BF16)


def dot(a, b):
    return jnp.dot(a, b, preferred_element_type=F32)


def left(weights, value):
    high, low = split(value)
    return dot(weights, jnp.concatenate([high, low, high], axis=0))


def right(value, high_w, low_w):
    high, low = split(value)
    return dot(high, high_w) + dot(low, high_w) + dot(high, low_w)


def tensor_kernel(unroll, ext, phases, table, wg, ws, zg, zs, cond, masked, along, smooth):
    gx, gy = lax.axis_index("gx"), lax.axis_index("gy")
    bx, by, z = cond.shape
    size_x, size_y = bx * lax.axis_size("gx"), by * lax.axis_size("gy")
    wide_y = ext.shape[1]
    rows_x = bx + 2 * SMOOTH

    row_y = gy * by - IMG_Y + lax.broadcasted_iota(jnp.int32, (wide_y, wg.shape[1]), 0)
    inside = jnp.logical_and(row_y >= 0, row_y < size_y)
    for k in range(2):
        part = wg[k * wide_y:(k + 1) * wide_y].astype(F32)
        masked[k * wide_y:(k + 1) * wide_y] = jnp.where(inside, part, 0.0).astype(BF16)

    def derive(step, carry):
        firsts, seconds = [], []
        for j in range(unroll):
            r = step * unroll + j
            at = gx * bx + r - SMOOTH
            ok = jnp.logical_and(at >= 0, at < size_x).astype(F32)
            e = [ext[r + t] for t in range(2 * DERIV + 1)]
            a = e[DERIV] * (NEAR[DERIV] * ok)
            b = jnp.zeros_like(a)
            for t in range(1, DERIV + 1):
                a = a + (e[DERIV + t] + e[DERIV - t]) * (NEAR[DERIV + t] * ok)
                b = b + (e[DERIV + t] - e[DERIV - t]) * (SLOPE[DERIV + t] * ok)
            y_a = left(masked[...], a)
            y_b = left(masked[:wide_y], b)
            firsts += [y_b, y_a[wide_y:]]
            seconds.append(y_a[:wide_y])
        first = right(jnp.concatenate(firsts, axis=0), zg[:, :z], zg[:, z:2 * z])
        second = right(jnp.concatenate(seconds, axis=0), zg[:, 2 * z:3 * z], zg[:, 3 * z:])
        for j in range(unroll):
            r = step * unroll + j
            g_x = first[2 * j * wide_y:(2 * j + 1) * wide_y]
            g_y = first[(2 * j + 1) * wide_y:(2 * j + 2) * wide_y]
            g_z = second[j * wide_y:(j + 1) * wide_y]
            for f, (p, q) in enumerate(
                ((g_x, g_x), (g_y, g_y), (g_z, g_z), (g_x, g_y), (g_x, g_z), (g_y, g_z))
            ):
                along[f, r] = left(ws[...], p * q)
        return carry

    lax.fori_loop(0, rows_x // unroll, derive, 0)

    tiles_y, tiles_z = by // 8, z // 128

    def smooth_x(step, carry):
        f = step // (tiles_y * tiles_z)
        ys = pl.ds(pl.multiple_of((step // tiles_z) % tiles_y * 8, 8), 8)
        zz = pl.ds(pl.multiple_of(step % tiles_z * 128, 128), 128)
        v = [along[f, r, ys, zz] for r in range(rows_x)]
        for i in range(bx):
            c = i + SMOOTH
            total = v[c] * WIDE[SMOOTH]
            for t in range(1, SMOOTH + 1):
                total = total + (v[c + t] + v[c - t]) * WIDE[SMOOTH + t]
            smooth[f, i, ys, zz] = total
        return carry

    lax.fori_loop(0, 6 * tiles_y * tiles_z, smooth_x, 0)

    def finish(i, carry):
        s = right(
            jnp.concatenate([smooth[f, i] for f in range(6)], axis=0), zs[:, :z], zs[:, z:])
        jxx, jyy, jzz, jxy, jxz, jyz = (s[f * by:(f + 1) * by] for f in range(6))
        trace = jxx + jyy + jzz
        shift = 0.1 * trace + 1e-06
        a, b, c = jxx + shift, jyy + shift, jzz + shift
        cof = a * b - jxy * jxy
        det = (
            a * (b * c - jyz * jyz)
            - jxy * (jxy * c - jyz * jxz)
            + jxz * (jxy * jyz - b * jxz)
        )
        weight = trace * cof / det
        label = phases[i]
        base = jnp.where(label == 0, table[0, 0], jnp.where(label == 1, table[0, 1], table[0, 2]))
        aniso = jnp.where(label == 0, table[1, 0], jnp.where(label == 1, table[1, 1], table[1, 2]))
        cond[i] = base + 0.1 * aniso * weight
        return carry

    lax.fori_loop(0, bx, finish, 0)


def tensor(ext, phases, table):
    bx, by, z = phases.shape
    wide_y = by + 2 * IMG_Y
    rows_x = bx + 2 * SMOOTH
    lo, hi = IMG_Y - SMOOTH, wide_y - (IMG_Y - SMOOTH)
    wg = np.concatenate([
        left_weights(band(wide_y, wide_y, 0, NEAR, lo, hi)),
        left_weights(band(wide_y, wide_y, 0, SLOPE, lo, hi)),
    ], axis=0)
    ws = left_weights(band(by, wide_y, IMG_Y, WIDE))
    zg = right_weights(band(z, z, 0, NEAR), band(z, z, 0, SLOPE))
    zs = right_weights(band(z, z, 0, WIDE))
    vmem = pl.BlockSpec(memory_space=pltpu.VMEM)
    return pl.pallas_call(
        functools.partial(tensor_kernel, 4),
        out_shape=jax.ShapeDtypeStruct((bx, by, z), F32),
        in_specs=[vmem, vmem, pl.BlockSpec(memory_space=pltpu.SMEM)] + [vmem] * 4,
        out_specs=vmem,
        scratch_shapes=[
            pltpu.VMEM(wg.shape, BF16),
            pltpu.VMEM((6, rows_x, by, z), F32),
            pltpu.VMEM((6, bx, by, z), F32),
        ],
        compiler_params=pltpu.CompilerParams(vmem_limit_bytes=48 * 1024 * 1024),
    )(ext, phases, table, wg, ws, zg, zs)


def harmonic(p, q):
    total = p + q
    return 2.0 * p * q / jnp.where(total > 0, total, 1.0)


def sweep_kernel(cond, start, out, kx, ky, k0, k1, inv, one, two):
    rows, wide, z = cond.shape
    lane = lax.broadcasted_iota(jnp.int32, (wide, z), 1)
    at_low, at_high = lane == 0, lane == z - 1

    def roll_y(v, s):
        return pltpu.roll(v, s % wide, 0)

    def roll_z(v, s):
        return pltpu.roll(v, s % z, 1)

    kx[0] = harmonic(cond[0], cond[1])

    def coefficients(j, carry):
        c = cond[j]
        upper = harmonic(c, cond[j + 1])
        kx[j] = upper
        y_up = harmonic(c, roll_y(c, -1))
        ky[j] = y_up
        z_up = harmonic(c, roll_z(c, -1))
        low = jnp.where(at_low, c, roll_z(z_up, 1))
        high = jnp.where(at_high, c, z_up)
        k0[j] = low
        k1[j] = high
        total = kx[j - 1] + upper + roll_y(y_up, 1) + y_up + low + high
        inv[j] = 1.0 / jnp.where(total > 0, total, 1.0)
        return carry

    lax.fori_loop(1, rows - 1, coefficients, 0)

    def sweep(src, dst, first, last):
        def step(j, carry):
            p = src[j]
            y_up = ky[j]
            numer = kx[j - 1] * src[j - 1] + kx[j] * src[j + 1]
            numer = numer + roll_y(y_up, 1) * roll_y(p, 1) + y_up * roll_y(p, -1)
            numer = numer + k0[j] * jnp.where(at_low, 1.0, roll_z(p, 1))
            numer = numer + k1[j] * jnp.where(at_high, 0.0, roll_z(p, -1))
            dst(j, numer * inv[j])
            return carry
        lax.fori_loop(first, last, step, 0)

    def into(ref):
        def put(j, v):
            ref[j] = v
        return put

    def put_out(j, v):
        out[j - POT_X] = v[POT_Y:wide - POT_Y]

    sweep(start, into(one), 1, rows - 1)
    sweep(one, into(two), 2, rows - 2)
    sweep(two, put_out, 3, rows - 3)


def sweeps(cond_ext, pot_ext):
    rows, wide, z = cond_ext.shape
    vmem = pl.BlockSpec(memory_space=pltpu.VMEM)
    return pl.pallas_call(
        sweep_kernel,
        out_shape=jax.ShapeDtypeStruct((rows - 2 * POT_X, wide - 2 * POT_Y, z), F32),
        in_specs=[vmem, vmem],
        out_specs=vmem,
        scratch_shapes=[pltpu.VMEM((rows, wide, z), F32)] * 7,
        compiler_params=pltpu.CompilerParams(vmem_limit_bytes=32 * 1024 * 1024),
    )(cond_ext, pot_ext)


def body(image, phases, phase_table, start_potential):
    image_cuts = ((0, 5), (5, 10), (10, 15))
    pot_cuts = ((0, 3),)
    (ext,) = exchange([image], [(IMG_X, IMG_Y, image_cuts)], 0)
    conductivity = tensor(ext, phases, phase_table)
    plan = (POT_X, POT_Y, pot_cuts)
    cond_ext, pot_ext = exchange([conductivity, start_potential], [plan, plan], 1)
    return conductivity, sweeps(cond_ext, pot_ext)


def solution(mesh):
    placed = (P("gx", "gy", None), P("gx", "gy", None), P(), P("gx", "gy", None))
    return jax.shard_map(
        body,
        mesh=mesh,
        in_specs=placed,
        out_specs=(P("gx", "gy", None), P("gx", "gy", None)),
        check_vma=False,
    )
```

profile of v0, /device:TPU:1, one launch (start us, length us, event | category | flops | bytes accessed | tf_op | source)
XLA Modules:
  0.0 67.6 jit_solution(971138192510093050)
XLA Ops:
  0.6 0.0 copy-start.1
  0.6 1.0 %copy-done.1 = f32[16,32,256]{2,1,0:T(8,128)S(1)} copy-done((f32[16,32,256]{2,1,0:T(8,128)S(1)}, f32[16,32,256]{2,1,0:T(8,128)}, u32[]{:S(2)}) %copy-start.1) | copy-done | bytes 524312
  1.7 0.0 copy-start.3
  1.7 0.0 copy-start.4
  1.7 0.0 copy-start.5
  1.7 0.0 copy-start.6
  1.7 0.0 copy-start.7
  1.7 0.0 copy-start.8
  1.7 19.7 %shard_map.95.ext = f32[46,64,256]{2,1,0:T(8,128)S(1)} custom-call(f32[16,32,256]{2,1,0:T(8,128)S(1)} %copy-done.1), custom_call_target="tpu_custom_call" | custom-call | tf_op jit(solution)/shard_map/pallas_call | solution.py:211
  21.4 0.0 copy-done.3
  21.4 0.0 copy-done.4
  21.4 0.0 copy-done.5
  21.4 0.0 copy-done.6
  21.5 0.0 copy-done.7
  21.5 0.0 copy-done.8
  21.5 0.0 copy-start.2
  21.5 23.9 %shard_map.96.refs_0_ = f32[16,32,256]{2,1,0:T(8,128)} custom-call(f32[46,64,256]{2,1,0:T(8,128)S(1)} %shard_map.95.ext, s32[16,32,256]{2,1,0:T(8,128)S(1)} %copy-done.3, f32[2,3]{1,0:T(2,128)S(1)} %copy-done.8, bf16[128,192]{1,0:T(8,128)(2,1)S(1)} %copy-done.6, bf16[32,192]{1,0:T(8,128)(2,1)S(1)} %copy-done.7, bf16[256,1024]{1,0:T(8,128)(2,1)S(1)} %copy-done.4, ...), custom_call_target="tpu_custom_call" | custom-call | tf_op jit(solution)/shard_map/pallas_call | solution.py:339
  45.3 0.0 copy-done.2
  45.3 0.0 copy-start
  45.3 1.0 %copy-done = f32[16,32,256]{2,1,0:T(8,128)S(1)} copy-done((f32[16,32,256]{2,1,0:T(8,128)S(1)}, f32[16,32,256]{2,1,0:T(8,128)}, u32[]{:S(2)}) %copy-start) | copy-done | bytes 524312
  46.4 11.6 %shard_map.97 = (f32[22,48,256]{2,1,0:T(8,128)S(1)}, f32[22,48,256]{2,1,0:T(8,128)S(1)}) custom-call(f32[16,32,256]{2,1,0:T(8,128)S(1)} %copy-done, f32[16,32,256]{2,1,0:T(8,128)S(1)} %copy-done.2), custom_call_target="tpu_custom_call" | custom-call | tf_op jit(solution)/shard_map/pallas_call | solution.py:211
  58.0 9.5 %shard_map.98 = f32[16,32,256]{2,1,0:T(8,128)} custom-call(f32[22,48,256]{2,1,0:T(8,128)S(1)} %get-tuple-element.4.cond, f32[22,48,256]{2,1,0:T(8,128)S(1)} %get-tuple-element.5.start), custom_call_target="tpu_custom_call" | custom-call | tf_op jit(solution)/shard_map/pallas_call | solution.py:416
Async XLA Ops:
  0.6 1.0 %copy-start.1 = (f32[16,32,256]{2,1,0:T(8,128)S(1)}, f32[16,32,256]{2,1,0:T(8,128)}, u32[]{:S(2)}) copy-start(f32[16,32,256]{2,1,0:T(8,128)} %refs_0_.1) | copy-start | bytes 1572868
  1.7 19.7 %copy-start.3 = (s32[16,32,256]{2,1,0:T(8,128)S(1)}, s32[16,32,256]{2,1,0:T(8,128)}, u32[]{:S(2)}) copy-start(s32[16,32,256]{2,1,0:T(8,128)} %phases.1) | copy-start | bytes 1572868
  1.7 19.8 %copy-start.4 = (bf16[256,1024]{1,0:T(8,128)(2,1)S(1)}, bf16[256,1024]{1,0:T(8,128)(2,1)}, u32[]{:S(2)}) copy-start(bf16[256,1024]{1,0:T(8,128)(2,1)} %constant.10.clone.zg) | copy-start | bytes 1572868
  1.7 19.8 %copy-start.5 = (bf16[256,512]{1,0:T(8,128)(2,1)S(1)}, bf16[256,512]{1,0:T(8,128)(2,1)}, u32[]{:S(2)}) copy-start(bf16[256,512]{1,0:T(8,128)(2,1)} %constant.11.clone.zs) | copy-start | bytes 786436
  1.7 19.8 %copy-start.6 = (bf16[128,192]{1,0:T(8,128)(2,1)S(1)}, bf16[128,192]{1,0:T(8,128)(2,1)}, u32[]{:S(2)}) copy-start(bf16[128,192]{1,0:T(8,128)(2,1)} %constant.8.clone.wg) | copy-start | bytes 147460
  1.7 19.8 %copy-start.7 = (bf16[32,192]{1,0:T(8,128)(2,1)S(1)}, bf16[32,192]{1,0:T(8,128)(2,1)}, u32[]{:S(2)}) copy-start(bf16[32,192]{1,0:T(8,128)(2,1)} %constant.9.clone.ws) | copy-start | bytes 36868
  1.7 19.8 %copy-start.8 = (f32[2,3]{1,0:T(2,128)S(1)}, f32[2,3]{1,0:T(2,128)}, u32[]{:S(2)}) copy-start(f32[2,3]{1,0:T(2,128)} %table.1) | copy-start | bytes 76
  21.5 23.9 %copy-start.2 = (f32[16,32,256]{2,1,0:T(8,128)S(1)}, f32[16,32,256]{2,1,0:T(8,128)}, u32[]{:S(2)}) copy-start(f32[16,32,256]{2,1,0:T(8,128)} %refs_1_.1) | copy-start | bytes 1572868
  45.3 1.0 %copy-start = (f32[16,32,256]{2,1,0:T(8,128)S(1)}, f32[16,32,256]{2,1,0:T(8,128)}, u32[]{:S(2)}) copy-start(f32[16,32,256]{2,1,0:T(8,128)} %shard_map.96.refs_0_) | copy-start | bytes 1572868
where the time goes:
time: 68.3 us; the launch traced here: 67.6 us
  Pallas kernels  64.7 us (95%)
  local copies, waits for them, and re-layouts  2.11 us (3%)
  between operations  0.73 us (1%)
    pallas_call x2, Pallas kernels, exchange(): pl.pallas_call(functools.partial(exchange_kernel, plans), out_shape=shape...  31.3 us
    pallas_call x1, Pallas kernels, tensor(): pl.pallas_call(functools.partial(tensor_kernel, 4), out_shape=jax.ShapeDt...  23.9 us
    pallas_call x1, Pallas kernels, sweeps(): pl.pallas_call(sweep_kernel, out_shape=jax.ShapeDtypeStruct((rows - 2 * P...  9.55 us
    unnamed x18, local copies, waits for them, and re-layouts  2.11 us

commit v1 on v0

--- a/solution.py
+++ b/solution.py
@@ -87,20 +87,26 @@
 
 
 class Exchange:
-    def __init__(self, own, ext, hx, hy, cuts, send, recv, local):
-        self.own, self.ext, self.hx, self.hy, self.cuts = own, ext, hx, hy, cuts
-        self.send, self.recv, self.local = send, recv, local
-        self.nx, self.ny = own.shape[0], own.shape[1]
+    def __init__(self, own, ext, hx, hy, cuts, bands, send, recv):
+        self.ext, self.hx, self.hy, self.cuts, self.bands = ext, hx, hy, cuts, bands
+        self.send, self.recv = send, recv
+        self.nx, self.ny = ext.shape[0] - 2 * hx, ext.shape[1] - 2 * hy
+        self.own = own
         self.has_x, self.has_y, self.at_x, self.at_y = neighbours()
 
     @staticmethod
-    def count(cuts):
-        return 2 + 6 * len(cuts)
+    def count(cuts, bands):
+        return 2 * len(bands) + 6 * len(cuts)
 
     def remote(self, src, dst, index, at):
         return pltpu.make_async_remote_copy(
             src_ref=src, dst_ref=dst, send_sem=self.send.at[index],
             recv_sem=self.recv.at[index], device_id=at, device_id_type=MESH)
+
+    def brick(self, row, rows, col, cols):
+        if self.own is None:
+            return self.ext.at[pl.ds(self.hx + row, rows), pl.ds(self.hy + col, cols)]
+        return self.own.at[pl.ds(row, rows), pl.ds(col, cols)]
 
     def halo_rows(self, d, cut):
         a, b = cut
@@ -113,17 +119,18 @@
         row, size = self.halo_rows(d, (a, b))
         start = a if d == 0 else self.nx - b
         return self.remote(
-            self.own.at[pl.ds(start, size)],
+            self.brick(start, size, 0, self.ny),
             self.ext.at[pl.ds(row, size), pl.ds(self.hy, self.ny)],
-            2 + d * len(self.cuts) + c, self.at_x[d])
-
-    def copy_y(self, d):
+            d * len(self.cuts) + c, self.at_x[d])
+
+    def copy_y(self, d, k):
+        a, b = self.bands[k]
         src = 0 if d == 0 else self.ny - self.hy
         dst = self.hy + self.ny if d == 0 else 0
         return self.remote(
-            self.own.at[:, pl.ds(src, self.hy)],
-            self.ext.at[pl.ds(self.hx, self.nx), pl.ds(dst, self.hy)],
-            d, self.at_y[d])
+            self.brick(a, b - a, src, self.hy),
+            self.ext.at[pl.ds(self.hx + a, b - a), pl.ds(dst, self.hy)],
+            6 * len(self.cuts) + d * len(self.bands) + k, self.at_y[d])
 
     def copy_corner(self, side, d, c):
         row, size = self.halo_rows(side, self.cuts[c])
@@ -133,19 +140,17 @@
         return self.remote(
             self.ext.at[pl.ds(row, size), pl.ds(src, self.hy)],
             self.ext.at[pl.ds(row, size), pl.ds(dst, self.hy)],
-            2 + 2 * n + (side * 2 + d) * n + c, self.at_y[d])
-
-    def copy_own(self):
-        return pltpu.make_async_copy(
-            self.own, self.ext.at[pl.ds(self.hx, self.nx), pl.ds(self.hy, self.ny)], self.local)
-
-    def start(self):
-        for c in range(len(self.cuts)):
-            for d in range(2):
-                pl.when(self.has_x[d])(lambda d=d, c=c: self.copy_x(d, c).start())
+            2 * n + (side * 2 + d) * n + c, self.at_y[d])
+
+    def start_x(self, c):
         for d in range(2):
-            pl.when(self.has_y[d])(lambda d=d: self.copy_y(d).start())
-        self.copy_own().start()
+            pl.when(self.has_x[d])(lambda d=d: self.copy_x(d, c).start())
+
+    def start_y(self, k):
+        for d in range(2):
+            pl.when(self.has_y[d])(lambda d=d: self.copy_y(d, k).start())
+
+    def clear(self):
         rows, cols, z = self.ext.shape
         for d in range(2):
             @pl.when(jnp.logical_not(self.has_x[d]))
@@ -158,26 +163,28 @@
                 at = 0 if d == 0 else self.hy + self.ny
                 self.ext[:, pl.ds(at, self.hy)] = jnp.zeros((rows, self.hy, z), F32)
 
-    def forward(self):
-        for c in range(len(self.cuts)):
-            for side in range(2):
-                @pl.when(self.has_x[1 - side])
-                def _(side=side, c=c):
-                    self.copy_x(side, c).wait_recv()
-                    for d in range(2):
-                        pl.when(self.has_y[d])(
-                            lambda d=d: self.copy_corner(side, d, c).start())
-
-    def finish(self):
-        self.copy_own().wait()
+    def forward(self, c):
+        for side in range(2):
+            @pl.when(self.has_x[1 - side])
+            def _(side=side):
+                self.copy_x(side, c).wait_recv()
+                for d in range(2):
+                    pl.when(self.has_y[d])(lambda d=d: self.copy_corner(side, d, c).start())
+
+    def wait_y(self, k):
         for d in range(2):
-            pl.when(self.has_y[1 - d])(lambda d=d: self.copy_y(d).wait_recv())
-            for c in range(len(self.cuts)):
-                for side in range(2):
-                    pl.when(jnp.logical_and(self.has_x[1 - side], self.has_y[1 - d]))(
-                        lambda d=d, c=c, side=side: self.copy_corner(side, d, c).wait_recv())
+            pl.when(self.has_y[1 - d])(lambda d=d: self.copy_y(d, k).wait_recv())
+
+    def wait_corner(self, c):
+        for side in range(2):
+            for d in range(2):
+                pl.when(jnp.logical_and(self.has_x[1 - side], self.has_y[1 - d]))(
+                    lambda d=d, side=side: self.copy_corner(side, d, c).wait_recv())
+
+    def wait_sends(self):
         for d in range(2):
-            pl.when(self.has_y[d])(lambda d=d: self.copy_y(d).wait_send())
+            for k in range(len(self.bands)):
+                pl.when(self.has_y[d])(lambda d=d, k=k: self.copy_y(d, k).wait_send())
             for c in range(len(self.cuts)):
                 pl.when(self.has_x[d])(lambda d=d, c=c: self.copy_x(d, c).wait_send())
                 for side in range(2):
@@ -185,41 +192,6 @@
                         lambda d=d, c=c, side=side: self.copy_corner(side, d, c).wait_send())
 
 
-def exchange_kernel(plans, *refs):
-    n = len(plans)
-    owns, exts, sems = refs[:n], refs[n:2 * n], refs[2 * n:]
-    greet()
-    parts = [
-        Exchange(own, ext, *plan, *sems[3 * i:3 * i + 3])
-        for i, (own, ext, plan) in enumerate(zip(owns, exts, plans))
-    ]
-    for part in parts:
-        part.start()
-    for part in parts:
-        part.forward()
-    for part in parts:
-        part.finish()
-
-
-def exchange(arrays, plans, collective_id):
-    shapes, scratch = [], []
-    for array, (hx, hy, cuts) in zip(arrays, plans):
-        x, y, z = array.shape
-        shapes.append(jax.ShapeDtypeStruct((x + 2 * hx, y + 2 * hy, z), F32))
-        count = Exchange.count(cuts)
-        scratch += [pltpu.SemaphoreType.DMA((count,))] * 2 + [pltpu.SemaphoreType.DMA]
-    return pl.pallas_call(
-        functools.partial(exchange_kernel, plans),
-        out_shape=shapes,
-        in_specs=[pl.BlockSpec(memory_space=pl.ANY)] * len(arrays),
-        out_specs=[pl.BlockSpec(memory_space=pltpu.VMEM)] * len(arrays),
-        scratch_shapes=scratch,
-        compiler_params=pltpu.CompilerParams(
-            collective_id=collective_id, has_side_effects=True,
-            vmem_limit_bytes=32 * 1024 * 1024),
-    )(*arrays)
-
-
 def split(value):
     high = value.astype(BF16)
     return high, (value - high.astype(F32)).astype(BF16)
@@ -239,23 +211,54 @@
     return dot(high, high_w) + dot(low, high_w) + dot(high, low_w)
 
 
-def tensor_kernel(unroll, ext, phases, table, wg, ws, zg, zs, cond, masked, along, smooth):
+STEP = 5
+IMG_CUTS = tuple((a, a + STEP) for a in range(0, IMG_X, STEP))
+POT_CUTS = ((0, POT_X),)
+
+
+def brick_bands(bx):
+    middle = bx // 2
+    return ((0, POT_X), (bx - POT_X, bx), (POT_X, middle), (middle, bx - POT_X))
+
+
+def tensor_kernel(image, phases, table, start, wg, ws, zg, zs, cond, pot,
+                  ext, masked, along, smooth, *sems):
     gx, gy = lax.axis_index("gx"), lax.axis_index("gy")
-    bx, by, z = cond.shape
+    bx, by, z = phases.shape
     size_x, size_y = bx * lax.axis_size("gx"), by * lax.axis_size("gy")
     wide_y = ext.shape[1]
     rows_x = bx + 2 * SMOOTH
+    bands = brick_bands(bx)
+
+    img = Exchange(image, ext, IMG_X, IMG_Y, IMG_CUTS, ((0, bx),), *sems[0:2])
+    pots = Exchange(start, pot, POT_X, POT_Y, POT_CUTS, ((0, bx),), *sems[2:4])
+    conds = Exchange(None, cond, POT_X, POT_Y, POT_CUTS, bands, *sems[4:6])
+    own_image = pltpu.make_async_copy(
+        image, ext.at[pl.ds(IMG_X, bx), pl.ds(IMG_Y, by)], sems[6])
+    own_start = pltpu.make_async_copy(
+        start, pot.at[pl.ds(POT_X, bx), pl.ds(POT_Y, by)], sems[7])
+
+    own_image.start()
+    greet()
+    img.start_x(0)
+    img.start_y(0)
+    for c in range(1, len(IMG_CUTS)):
+        img.start_x(c)
+    own_start.start()
+    for part in (img, pots, conds):
+        part.clear()
 
     row_y = gy * by - IMG_Y + lax.broadcasted_iota(jnp.int32, (wide_y, wg.shape[1]), 0)
     inside = jnp.logical_and(row_y >= 0, row_y < size_y)
     for k in range(2):
         part = wg[k * wide_y:(k + 1) * wide_y].astype(F32)
         masked[k * wide_y:(k + 1) * wide_y] = jnp.where(inside, part, 0.0).astype(BF16)
-
-    def derive(step, carry):
+    own_image.wait()
+
+    def derive(row):
         firsts, seconds = [], []
-        for j in range(unroll):
-            r = step * unroll + j
+        for j in range(STEP):
+            r = row + j
             at = gx * bx + r - SMOOTH
             ok = jnp.logical_and(at >= 0, at < size_x).astype(F32)
             e = [ext[r + t] for t in range(2 * DERIV + 1)]
@@ -270,8 +273,8 @@
             seconds.append(y_a[:wide_y])
         first = right(jnp.concatenate(firsts, axis=0), zg[:, :z], zg[:, z:2 * z])
         second = right(jnp.concatenate(seconds, axis=0), zg[:, 2 * z:3 * z], zg[:, 3 * z:])
-        for j in range(unroll):
-            r = step * unroll + j
+        for j in range(STEP):
+            r = row + j
             g_x = first[2 * j * wide_y:(2 * j + 1) * wide_y]
             g_y = first[(2 * j + 1) * wide_y:(2 * j + 2) * wide_y]
             g_z = second[j * wide_y:(j + 1) * wide_y]
@@ -279,10 +282,26 @@
                 ((g_x, g_x), (g_y, g_y), (g_z, g_z), (g_x, g_y), (g_x, g_z), (g_y, g_z))
             ):
                 along[f, r] = left(ws[...], p * q)
-        return carry
-
-    lax.fori_loop(0, rows_x // unroll, derive, 0)
-
+
+    def derive_both(low, high):
+        def step(k, carry):
+            derive(low + k * (high - low))
+            return carry
+        lax.fori_loop(0, 2, step, 0)
+
+    centre = rows_x // 2
+    img.forward(0)
+    img.wait_y(0)
+    img.forward(1)
+    derive_both(centre - STEP, centre)
+    img.forward(2)
+    pots.start_x(0)
+    pots.start_y(0)
+    for c in range(len(IMG_CUTS)):
+        img.wait_corner(c)
+        derive_both(centre - (c + 2) * STEP, centre + (c + 1) * STEP)
+
+    pots.forward(0)
     tiles_y, tiles_z = by // 8, z // 128
 
     def smooth_x(step, carry):
@@ -317,13 +336,29 @@
         label = phases[i]
         base = jnp.where(label == 0, table[0, 0], jnp.where(label == 1, table[0, 1], table[0, 2]))
         aniso = jnp.where(label == 0, table[1, 0], jnp.where(label == 1, table[1, 1], table[1, 2]))
-        cond[i] = base + 0.1 * aniso * weight
+        cond[POT_X + i, POT_Y:POT_Y + by] = base + 0.1 * aniso * weight
         return carry
 
-    lax.fori_loop(0, bx, finish, 0)
-
-
-def tensor(ext, phases, table):
+    for k, (low, high) in enumerate(bands):
+        lax.fori_loop(low, high, finish, 0)
+        if k == 1:
+            conds.start_x(0)
+            conds.start_y(0)
+        if k >= 1:
+            conds.start_y(k)
+    conds.forward(0)
+
+    own_start.wait()
+    pots.wait_y(0)
+    pots.wait_corner(0)
+    for k in range(len(bands)):
+        conds.wait_y(k)
+    conds.wait_corner(0)
+    for part in (img, pots, conds):
+        part.wait_sends()
+
+
+def tensor(image, phases, table, start):
     bx, by, z = phases.shape
     wide_y = by + 2 * IMG_Y
     rows_x = bx + 2 * SMOOTH
@@ -336,18 +371,29 @@
     zg = right_weights(band(z, z, 0, NEAR), band(z, z, 0, SLOPE))
     zs = right_weights(band(z, z, 0, WIDE))
     vmem = pl.BlockSpec(memory_space=pltpu.VMEM)
+    hbm = pl.BlockSpec(memory_space=pltpu.HBM)
+    outer = jax.ShapeDtypeStruct((bx + 2 * POT_X, by + 2 * POT_Y, z), F32)
+    sems = []
+    for count in (
+        Exchange.count(IMG_CUTS, ((0, bx),)),
+        Exchange.count(POT_CUTS, ((0, bx),)),
+        Exchange.count(POT_CUTS, brick_bands(bx)),
+    ):
+        sems += [pltpu.SemaphoreType.DMA((count,))] * 2
     return pl.pallas_call(
-        functools.partial(tensor_kernel, 4),
-        out_shape=jax.ShapeDtypeStruct((bx, by, z), F32),
-        in_specs=[vmem, vmem, pl.BlockSpec(memory_space=pltpu.SMEM)] + [vmem] * 4,
-        out_specs=vmem,
+        tensor_kernel,
+        out_shape=[outer, outer],
+        in_specs=[hbm, vmem, pl.BlockSpec(memory_space=pltpu.SMEM), hbm] + [vmem] * 4,
+        out_specs=[vmem, vmem],
         scratch_shapes=[
+            pltpu.VMEM((bx + 2 * IMG_X, wide_y, z), F32),
             pltpu.VMEM(wg.shape, BF16),
             pltpu.VMEM((6, rows_x, by, z), F32),
             pltpu.VMEM((6, bx, by, z), F32),
-        ],
-        compiler_params=pltpu.CompilerParams(vmem_limit_bytes=48 * 1024 * 1024),
-    )(ext, phases, table, wg, ws, zg, zs)
+        ] + sems + [pltpu.SemaphoreType.DMA] * 2,
+        compiler_params=pltpu.CompilerParams(
+            collective_id=0, has_side_effects=True, vmem_limit_bytes=44 * 1024 * 1024),
+    )(image, phases, table, start, wg, ws, zg, zs)
 
 
 def harmonic(p, q):
@@ -355,8 +401,11 @@
     return 2.0 * p * q / jnp.where(total > 0, total, 1.0)
 
 
-def sweep_kernel(cond, start, out, kx, ky, k0, k1, inv, one, two):
+def sweep_kernel(cond, start, centre, out, kx, ky, k0, k1, inv, one, two, sem):
     rows, wide, z = cond.shape
+    copy = pltpu.make_async_copy(
+        cond.at[pl.ds(POT_X, rows - 2 * POT_X), pl.ds(POT_Y, wide - 2 * POT_Y)], centre, sem)
+    copy.start()
     lane = lax.broadcasted_iota(jnp.int32, (wide, z), 1)
     at_low, at_high = lane == 0, lane == z - 1
 
@@ -408,29 +457,27 @@
     sweep(start, into(one), 1, rows - 1)
     sweep(one, into(two), 2, rows - 2)
     sweep(two, put_out, 3, rows - 3)
+    copy.wait()
 
 
 def sweeps(cond_ext, pot_ext):
     rows, wide, z = cond_ext.shape
     vmem = pl.BlockSpec(memory_space=pltpu.VMEM)
+    brick = jax.ShapeDtypeStruct((rows - 2 * POT_X, wide - 2 * POT_Y, z), F32)
     return pl.pallas_call(
         sweep_kernel,
-        out_shape=jax.ShapeDtypeStruct((rows - 2 * POT_X, wide - 2 * POT_Y, z), F32),
+        out_shape=[brick, brick],
         in_specs=[vmem, vmem],
-        out_specs=vmem,
-        scratch_shapes=[pltpu.VMEM((rows, wide, z), F32)] * 7,
+        out_specs=[pl.BlockSpec(memory_space=pltpu.HBM), vmem],
+        scratch_shapes=[pltpu.VMEM((rows, wide, z), F32)] * 7 + [pltpu.SemaphoreType.DMA],
         compiler_params=pltpu.CompilerParams(vmem_limit_bytes=32 * 1024 * 1024),
     )(cond_ext, pot_ext)
 
 
 def body(image, phases, phase_table, start_potential):
-    image_cuts = ((0, 5), (5, 10), (10, 15))
-    pot_cuts = ((0, 3),)
-    (ext,) = exchange([image], [(IMG_X, IMG_Y, image_cuts)], 0)
-    conductivity = tensor(ext, phases, phase_table)
-    plan = (POT_X, POT_Y, pot_cuts)
-    cond_ext, pot_ext = exchange([conductivity, start_potential], [plan, plan], 1)
-    return conductivity, sweeps(cond_ext, pot_ext)
+    cond_ext, pot_ext = tensor(image, phases, phase_table, start_potential)
+    conductivity, potential = sweeps(cond_ext, pot_ext)
+    return conductivity, potential
 
 
 def solution(mesh):

time: 68.3 us -> 59.2 us (0.87)
  Pallas kernels: 64.7 us -> 50.7 us
  local copies, waits for them, and re-layouts: 2.11 us -> 7.34 us
    pallas_call x4 -> x2, Pallas kernels: 64.7 us -> 50.7 us  [the longest x1 41 us: tensor(): pl.pallas_call(tensor_kernel, out_shape=[outer, outer], in_specs=[hbm, vm...]
    unnamed x18 -> x16, local copies, waits for them, and re-layouts: 2.11 us -> 7.34 us
where the time goes in v1:
time: 59.2 us; the launch traced here: 58.7 us
  Pallas kernels  50.7 us (86%)
  local copies, waits for them, and re-layouts  7.34 us (12%)
  between operations  0.65 us (1%)
    pallas_call x1, Pallas kernels, tensor(): pl.pallas_call(tensor_kernel, out_shape=[outer, outer], in_specs=[hbm, vm...  41 us
    pallas_call x1, Pallas kernels, sweeps(): pl.pallas_call(sweep_kernel, out_shape=[brick, brick], in_specs=[vmem, vm...  9.68 us
    unnamed x16, local copies, waits for them, and re-layouts  7.34 us

profile of v1, /device:TPU:1, one launch (start us, length us, event | category | flops | bytes accessed | tf_op | source)
XLA Modules:
  0.0 58.7 jit_solution(15006401224008065650)
XLA Ops:
  0.6 0.0 copy-start
  0.6 1.0 %copy-done = f32[16,32,256]{2,1,0:T(8,128)S(1)} copy-done((f32[16,32,256]{2,1,0:T(8,128)S(1)}, f32[16,32,256]{2,1,0:T(8,128)}, u32[]{:S(2)}) %copy-start) | copy-done | bytes 524312
  1.7 0.0 copy-start.1
  1.7 1.0 %copy-done.1 = s32[16,32,256]{2,1,0:T(8,128)S(1)} copy-done((s32[16,32,256]{2,1,0:T(8,128)S(1)}, s32[16,32,256]{2,1,0:T(8,128)}, u32[]{:S(2)}) %copy-start.1) | copy-done | bytes 524312
  2.7 0.0 copy-start.2
  2.7 1.0 %copy-done.2 = f32[16,32,256]{2,1,0:T(8,128)S(1)} copy-done((f32[16,32,256]{2,1,0:T(8,128)S(1)}, f32[16,32,256]{2,1,0:T(8,128)}, u32[]{:S(2)}) %copy-start.2) | copy-done | bytes 524312
  3.8 0.0 copy-start.3
  3.8 1.0 %copy-done.3 = bf16[256,1024]{1,0:T(8,128)(2,1)S(1)} copy-done((bf16[256,1024]{1,0:T(8,128)(2,1)S(1)}, bf16[256,1024]{1,0:T(8,128)(2,1)}, u32[]{:S(2)}) %copy-start.3) | copy-done | bytes 524312
  4.8 0.0 copy-start.4
  4.8 0.9 %copy-done.4 = bf16[256,512]{1,0:T(8,128)(2,1)S(1)} copy-done((bf16[256,512]{1,0:T(8,128)(2,1)S(1)}, bf16[256,512]{1,0:T(8,128)(2,1)}, u32[]{:S(2)}) %copy-start.4) | copy-done | bytes 262168
  5.8 0.0 copy-start.5
  5.8 0.8 %copy-done.5 = bf16[128,192]{1,0:T(8,128)(2,1)S(1)} copy-done((bf16[128,192]{1,0:T(8,128)(2,1)S(1)}, bf16[128,192]{1,0:T(8,128)(2,1)}, u32[]{:S(2)}) %copy-start.5) | copy-done | bytes 49176
  6.6 0.0 copy-start.6
  6.6 0.7 %copy-done.6 = bf16[32,192]{1,0:T(8,128)(2,1)S(1)} copy-done((bf16[32,192]{1,0:T(8,128)(2,1)S(1)}, bf16[32,192]{1,0:T(8,128)(2,1)}, u32[]{:S(2)}) %copy-start.6) | copy-done | bytes 12312
  7.3 0.0 copy-start.7
  7.3 0.7 %copy-done.7 = f32[2,3]{1,0:T(2,128)S(1)} copy-done((f32[2,3]{1,0:T(2,128)S(1)}, f32[2,3]{1,0:T(2,128)}, u32[]{:S(2)}) %copy-start.7) | copy-done | bytes 48
  8.0 41.0 %shard_map.95 = (f32[22,48,256]{2,1,0:T(8,128)S(1)}, f32[22,48,256]{2,1,0:T(8,128)S(1)}) custom-call(f32[16,32,256]{2,1,0:T(8,128)S(1)} %copy-done, s32[16,32,256]{2,1,0:T(8,128)S(1)} %copy-done.1, f32[2,3]{1,0:T(2,128)S(1)} %copy-done.7, f32[16,32,256]{2,1,0:T(8,128)S(1)} %copy-done.2, bf16[128,192]{1,0:T(8,128)(2,1)S(1)} %copy-done.5, ...), custom_call_target="tpu_custom_call" | custom-call | tf_op jit(solution)/shard_map/pallas_call | solution.py:383
  49.0 9.7 %shard_map.96 = (f32[16,32,256]{2,1,0:T(8,128)}, f32[16,32,256]{2,1,0:T(8,128)}) custom-call(f32[22,48,256]{2,1,0:T(8,128)S(1)} %get-tuple-element.4.cond, f32[22,48,256]{2,1,0:T(8,128)S(1)} %get-tuple-element.5.start), custom_call_target="tpu_custom_call" | custom-call | tf_op jit(solution)/shard_map/pallas_call | solution.py:467
Async XLA Ops:
  0.6 1.0 %copy-start = (f32[16,32,256]{2,1,0:T(8,128)S(1)}, f32[16,32,256]{2,1,0:T(8,128)}, u32[]{:S(2)}) copy-start(f32[16,32,256]{2,1,0:T(8,128)} %image.1) | copy-start | bytes 1572868
  1.7 1.0 %copy-start.1 = (s32[16,32,256]{2,1,0:T(8,128)S(1)}, s32[16,32,256]{2,1,0:T(8,128)}, u32[]{:S(2)}) copy-start(s32[16,32,256]{2,1,0:T(8,128)} %phases.1) | copy-start | bytes 1572868
  2.7 1.0 %copy-start.2 = (f32[16,32,256]{2,1,0:T(8,128)S(1)}, f32[16,32,256]{2,1,0:T(8,128)}, u32[]{:S(2)}) copy-start(f32[16,32,256]{2,1,0:T(8,128)} %start.1) | copy-start | bytes 1572868
  3.8 1.0 %copy-start.3 = (bf16[256,1024]{1,0:T(8,128)(2,1)S(1)}, bf16[256,1024]{1,0:T(8,128)(2,1)}, u32[]{:S(2)}) copy-start(bf16[256,1024]{1,0:T(8,128)(2,1)} %constant.10.clone.zg) | copy-start | bytes 1572868
  4.8 0.9 %copy-start.4 = (bf16[256,512]{1,0:T(8,128)(2,1)S(1)}, bf16[256,512]{1,0:T(8,128)(2,1)}, u32[]{:S(2)}) copy-start(bf16[256,512]{1,0:T(8,128)(2,1)} %constant.11.clone.zs) | copy-start | bytes 786436
  5.8 0.8 %copy-start.5 = (bf16[128,192]{1,0:T(8,128)(2,1)S(1)}, bf16[128,192]{1,0:T(8,128)(2,1)}, u32[]{:S(2)}) copy-start(bf16[128,192]{1,0:T(8,128)(2,1)} %constant.8.clone.wg) | copy-start | bytes 147460
  6.6 0.7 %copy-start.6 = (bf16[32,192]{1,0:T(8,128)(2,1)S(1)}, bf16[32,192]{1,0:T(8,128)(2,1)}, u32[]{:S(2)}) copy-start(bf16[32,192]{1,0:T(8,128)(2,1)} %constant.9.clone.ws) | copy-start | bytes 36868
  7.3 0.7 %copy-start.7 = (f32[2,3]{1,0:T(2,128)S(1)}, f32[2,3]{1,0:T(2,128)}, u32[]{:S(2)}) copy-start(f32[2,3]{1,0:T(2,128)} %table.1) | copy-start | bytes 76

commit v2 on v1

--- a/solution.py
+++ b/solution.py
@@ -19,6 +19,7 @@
 POT_X = SWEEPS
 POT_Y = 8
 MESH = pl.DeviceIdType.MESH
+VMEM_LIMIT = 58 * 1024 * 1024
 F32 = jnp.float32
 BF16 = jnp.bfloat16
 
@@ -221,8 +222,8 @@
     return ((0, POT_X), (bx - POT_X, bx), (POT_X, middle), (middle, bx - POT_X))
 
 
-def tensor_kernel(image, phases, table, start, wg, ws, zg, zs, cond, pot,
-                  ext, masked, along, smooth, *sems):
+def tensor_kernel(image, phases_in, table_in, start, wg_in, ws_in, zg_in, zs_in, cond, pot,
+                  ext, masked, along, smooth, phases, table, wg, ws, zg, zs, *sems):
     gx, gy = lax.axis_index("gx"), lax.axis_index("gy")
     bx, by, z = phases.shape
     size_x, size_y = bx * lax.axis_size("gx"), by * lax.axis_size("gy")
@@ -238,7 +239,15 @@
     own_start = pltpu.make_async_copy(
         start, pot.at[pl.ds(POT_X, bx), pl.ds(POT_Y, by)], sems[7])
 
+    loads = [
+        pltpu.make_async_copy(src, dst, sems[8 + k])
+        for k, (src, dst) in enumerate((
+            (wg_in, wg), (zg_in, zg), (ws_in, ws), (phases_in, phases), (zs_in, zs),
+            (table_in, table)))
+    ]
     own_image.start()
+    for load in loads:
+        load.start()
     greet()
     img.start_x(0)
     img.start_y(0)
@@ -248,6 +257,8 @@
     for part in (img, pots, conds):
         part.clear()
 
+    for load in loads[:3]:
+        load.wait()
     row_y = gy * by - IMG_Y + lax.broadcasted_iota(jnp.int32, (wide_y, wg.shape[1]), 0)
     inside = jnp.logical_and(row_y >= 0, row_y < size_y)
     for k in range(2):
@@ -302,6 +313,8 @@
         derive_both(centre - (c + 2) * STEP, centre + (c + 1) * STEP)
 
     pots.forward(0)
+    for load in loads[3:]:
+        load.wait()
     tiles_y, tiles_z = by // 8, z // 128
 
     def smooth_x(step, carry):
@@ -371,7 +384,7 @@
     zg = right_weights(band(z, z, 0, NEAR), band(z, z, 0, SLOPE))
     zs = right_weights(band(z, z, 0, WIDE))
     vmem = pl.BlockSpec(memory_space=pltpu.VMEM)
-    hbm = pl.BlockSpec(memory_space=pltpu.HBM)
+    anywhere = pl.BlockSpec(memory_space=pl.ANY)
     outer = jax.ShapeDtypeStruct((bx + 2 * POT_X, by + 2 * POT_Y, z), F32)
     sems = []
     for count in (
@@ -383,16 +396,19 @@
     return pl.pallas_call(
         tensor_kernel,
         out_shape=[outer, outer],
-        in_specs=[hbm, vmem, pl.BlockSpec(memory_space=pltpu.SMEM), hbm] + [vmem] * 4,
+        in_specs=[anywhere] * 8,
         out_specs=[vmem, vmem],
         scratch_shapes=[
             pltpu.VMEM((bx + 2 * IMG_X, wide_y, z), F32),
             pltpu.VMEM(wg.shape, BF16),
             pltpu.VMEM((6, rows_x, by, z), F32),
             pltpu.VMEM((6, bx, by, z), F32),
-        ] + sems + [pltpu.SemaphoreType.DMA] * 2,
+            pltpu.VMEM(phases.shape, jnp.int32),
+            pltpu.SMEM(table.shape, F32),
+        ] + [pltpu.VMEM(w.shape, BF16) for w in (wg, ws, zg, zs)]
+        + sems + [pltpu.SemaphoreType.DMA] * 8,
         compiler_params=pltpu.CompilerParams(
-            collective_id=0, has_side_effects=True, vmem_limit_bytes=44 * 1024 * 1024),
+            collective_id=0, has_side_effects=True, vmem_limit_bytes=VMEM_LIMIT),
     )(image, phases, table, start, wg, ws, zg, zs)
 
 
@@ -401,58 +417,67 @@
     return 2.0 * p * q / jnp.where(total > 0, total, 1.0)
 
 
-def sweep_kernel(cond, start, centre, out, kx, ky, k0, k1, inv, one, two, sem):
+PAIR = 2
+
+
+def sweep_kernel(cond, start, centre, out, kx, y0, y1, z0, z1, inv, one, two, sem):
     rows, wide, z = cond.shape
     copy = pltpu.make_async_copy(
         cond.at[pl.ds(POT_X, rows - 2 * POT_X), pl.ds(POT_Y, wide - 2 * POT_Y)], centre, sem)
     copy.start()
-    lane = lax.broadcasted_iota(jnp.int32, (wide, z), 1)
+    lane = lax.broadcasted_iota(jnp.int32, (PAIR, wide, z), 2)
     at_low, at_high = lane == 0, lane == z - 1
 
     def roll_y(v, s):
-        return pltpu.roll(v, s % wide, 0)
+        return pltpu.roll(v, s % wide, 1)
 
     def roll_z(v, s):
-        return pltpu.roll(v, s % z, 1)
+        return pltpu.roll(v, s % z, 2)
 
     kx[0] = harmonic(cond[0], cond[1])
 
-    def coefficients(j, carry):
-        c = cond[j]
-        upper = harmonic(c, cond[j + 1])
-        kx[j] = upper
+    def coefficients(step, carry):
+        j = 1 + step * PAIR
+        c = cond[pl.ds(j, PAIR)]
+        x_up = harmonic(c, cond[pl.ds(j + 1, PAIR)])
         y_up = harmonic(c, roll_y(c, -1))
-        ky[j] = y_up
         z_up = harmonic(c, roll_z(c, -1))
+        x_down = jnp.concatenate([kx[j - 1][None], x_up[:PAIR - 1]], axis=0)
+        y_down = roll_y(y_up, 1)
         low = jnp.where(at_low, c, roll_z(z_up, 1))
         high = jnp.where(at_high, c, z_up)
-        k0[j] = low
-        k1[j] = high
-        total = kx[j - 1] + upper + roll_y(y_up, 1) + y_up + low + high
-        inv[j] = 1.0 / jnp.where(total > 0, total, 1.0)
+        total = x_down + x_up + y_down + y_up + low + high
+        kx[pl.ds(j, PAIR)] = x_up
+        y0[pl.ds(j, PAIR)] = y_down
+        y1[pl.ds(j, PAIR)] = y_up
+        z0[pl.ds(j, PAIR)] = low
+        z1[pl.ds(j, PAIR)] = high
+        inv[pl.ds(j, PAIR)] = 1.0 / jnp.where(total > 0, total, 1.0)
         return carry
 
-    lax.fori_loop(1, rows - 1, coefficients, 0)
-
-    def sweep(src, dst, first, last):
-        def step(j, carry):
-            p = src[j]
-            y_up = ky[j]
-            numer = kx[j - 1] * src[j - 1] + kx[j] * src[j + 1]
-            numer = numer + roll_y(y_up, 1) * roll_y(p, 1) + y_up * roll_y(p, -1)
-            numer = numer + k0[j] * jnp.where(at_low, 1.0, roll_z(p, 1))
-            numer = numer + k1[j] * jnp.where(at_high, 0.0, roll_z(p, -1))
-            dst(j, numer * inv[j])
+    lax.fori_loop(0, (rows - 2) // PAIR, coefficients, 0)
+
+    def sweep(src, put, first, last):
+        def step(k, carry):
+            j = first + k * PAIR
+            at = pl.ds(j, PAIR)
+            p = src[at]
+            numer = kx[pl.ds(j - 1, PAIR)] * src[pl.ds(j - 1, PAIR)]
+            numer = numer + kx[at] * src[pl.ds(j + 1, PAIR)]
+            numer = numer + y0[at] * roll_y(p, 1) + y1[at] * roll_y(p, -1)
+            numer = numer + z0[at] * jnp.where(at_low, 1.0, roll_z(p, 1))
+            numer = numer + z1[at] * jnp.where(at_high, 0.0, roll_z(p, -1))
+            put(j, numer * inv[at])
             return carry
-        lax.fori_loop(first, last, step, 0)
+        lax.fori_loop(0, (last - first) // PAIR, step, 0)
 
     def into(ref):
         def put(j, v):
-            ref[j] = v
+            ref[pl.ds(j, PAIR)] = v
         return put
 
     def put_out(j, v):
-        out[j - POT_X] = v[POT_Y:wide - POT_Y]
+        out[pl.ds(j - POT_X, PAIR)] = v[:, POT_Y:wide - POT_Y]
 
     sweep(start, into(one), 1, rows - 1)
     sweep(one, into(two), 2, rows - 2)
@@ -469,7 +494,7 @@
         out_shape=[brick, brick],
         in_specs=[vmem, vmem],
         out_specs=[pl.BlockSpec(memory_space=pltpu.HBM), vmem],
-        scratch_shapes=[pltpu.VMEM((rows, wide, z), F32)] * 7 + [pltpu.SemaphoreType.DMA],
+        scratch_shapes=[pltpu.VMEM((rows, wide, z), F32)] * 8 + [pltpu.SemaphoreType.DMA],
         compiler_params=pltpu.CompilerParams(vmem_limit_bytes=32 * 1024 * 1024),
     )(cond_ext, pot_ext)
 

time: 59.2 us -> 51.6 us (0.87)
  local copies, waits for them, and re-layouts: 7.34 us -> 2.47 us
  Pallas kernels: 50.7 us -> 48.3 us
    unnamed x16 -> x4, local copies, waits for them, and re-layouts: 7.34 us -> 2.47 us
    pallas_call x1, Pallas kernels: 9.68 us -> 6.2 us  [sweeps(): pl.pallas_call(sweep_kernel, out_shape=[brick, brick], in_specs=[vmem, vm...]
    pallas_call x1, Pallas kernels: 41 us -> 42.1 us  [tensor(): pl.pallas_call(tensor_kernel, out_shape=[outer, outer], in_specs=[anywher...]
where the time goes in v2:
time: 51.6 us; the launch traced here: 51.4 us
  Pallas kernels  48.3 us (94%)
  local copies, waits for them, and re-layouts  2.47 us (5%)
  between operations  0.65 us (1%)
    pallas_call x1, Pallas kernels, tensor(): pl.pallas_call(tensor_kernel, out_shape=[outer, outer], in_specs=[anywher...  42.1 us
    pallas_call x1, Pallas kernels, sweeps(): pl.pallas_call(sweep_kernel, out_shape=[brick, brick], in_specs=[vmem, vm...  6.2 us
    unnamed x4, local copies, waits for them, and re-layouts  2.47 us

profile of v2, /device:TPU:1, one launch (start us, length us, event | category | flops | bytes accessed | tf_op | source)
XLA Modules:
  0.0 51.4 jit_solution(2241943966411664160)
XLA Ops:
  0.6 42.1 %shard_map.95 = (f32[22,48,256]{2,1,0:T(8,128)}, f32[22,48,256]{2,1,0:T(8,128)}) custom-call(f32[16,32,256]{2,1,0:T(8,128)} %image.1, s32[16,32,256]{2,1,0:T(8,128)} %phases_in.1, f32[2,3]{1,0:T(2,128)} %table_in.1, f32[16,32,256]{2,1,0:T(8,128)} %start.1, bf16[128,192]{1,0:T(8,128)(2,1)} %constant.8.clone.wg_in, bf16[32,192]{1,0:T(8,128)(2,1)} %constant.9.clone.ws_in, ...), custom_call_target="tpu_custom_call" | custom-call | tf_op jit(solution)/shard_map/pallas_call | solution.py:396
  42.7 0.0 copy-start
  42.7 1.2 %copy-done = f32[22,48,256]{2,1,0:T(8,128)S(1)} copy-done((f32[22,48,256]{2,1,0:T(8,128)S(1)}, f32[22,48,256]{2,1,0:T(8,128)}, u32[]{:S(2)}) %copy-start) | copy-done | bytes 1081368
  44.0 0.0 copy-start.1
  44.0 1.2 %copy-done.1 = f32[22,48,256]{2,1,0:T(8,128)S(1)} copy-done((f32[22,48,256]{2,1,0:T(8,128)S(1)}, f32[22,48,256]{2,1,0:T(8,128)}, u32[]{:S(2)}) %copy-start.1) | copy-done | bytes 1081368
  45.2 6.2 %shard_map.96 = (f32[16,32,256]{2,1,0:T(8,128)}, f32[16,32,256]{2,1,0:T(8,128)}) custom-call(f32[22,48,256]{2,1,0:T(8,128)S(1)} %copy-done, f32[22,48,256]{2,1,0:T(8,128)S(1)} %copy-done.1), custom_call_target="tpu_custom_call" | custom-call | tf_op jit(solution)/shard_map/pallas_call | solution.py:492
Async XLA Ops:
  42.7 1.2 %copy-start = (f32[22,48,256]{2,1,0:T(8,128)S(1)}, f32[22,48,256]{2,1,0:T(8,128)}, u32[]{:S(2)}) copy-start(f32[22,48,256]{2,1,0:T(8,128)} %get-tuple-element.4.cond) | copy-start | bytes 3244036
  44.0 1.2 %copy-start.1 = (f32[22,48,256]{2,1,0:T(8,128)S(1)}, f32[22,48,256]{2,1,0:T(8,128)}, u32[]{:S(2)}) copy-start(f32[22,48,256]{2,1,0:T(8,128)} %get-tuple-element.5.start) | copy-start | bytes 3244036

commit v3 on v2

--- a/solution.py
+++ b/solution.py
@@ -308,57 +308,75 @@
     img.forward(2)
     pots.start_x(0)
     pots.start_y(0)
-    for c in range(len(IMG_CUTS)):
+    tiles_y, tiles_z = by // 8, z // 128
+
+    def smooth_x(known, ready, add):
+        def step(n, carry):
+            f = n // (tiles_y * tiles_z)
+            ys = pl.ds(pl.multiple_of((n // tiles_z) % tiles_y * 8, 8), 8)
+            zz = pl.ds(pl.multiple_of(n % tiles_z * 128, 128), 128)
+            new = [r in known and r not in ready for r in range(rows_x)]
+            v = [along[f, r, ys, zz] if new[r] else None for r in range(rows_x)]
+            for i in range(bx):
+                c = i + SMOOTH
+                terms = [v[c] * WIDE[SMOOTH]] if new[c] else []
+                for t in range(1, SMOOTH + 1):
+                    pair = [v[r] for r in (c + t, c - t) if new[r]]
+                    if pair:
+                        terms.append((pair[0] + pair[1] if len(pair) > 1 else pair[0])
+                                     * WIDE[SMOOTH + t])
+                if terms:
+                    total = smooth[f, i, ys, zz] if add else terms.pop(0)
+                    for term in terms:
+                        total = total + term
+                    smooth[f, i, ys, zz] = total
+            return carry
+        lax.fori_loop(0, 6 * tiles_y * tiles_z, step, 0)
+
+    last = len(IMG_CUTS) - 1
+    for c in range(last):
         img.wait_corner(c)
         derive_both(centre - (c + 2) * STEP, centre + (c + 1) * STEP)
-
+    inner = range(STEP, rows_x - STEP)
+    smooth_x(inner, (), False)
+    img.wait_corner(last)
+    derive_both(0, rows_x - STEP)
     pots.forward(0)
+    smooth_x(range(rows_x), inner, True)
     for load in loads[3:]:
         load.wait()
-    tiles_y, tiles_z = by // 8, z // 128
-
-    def smooth_x(step, carry):
-        f = step // (tiles_y * tiles_z)
-        ys = pl.ds(pl.multiple_of((step // tiles_z) % tiles_y * 8, 8), 8)
-        zz = pl.ds(pl.multiple_of(step % tiles_z * 128, 128), 128)
-        v = [along[f, r, ys, zz] for r in range(rows_x)]
-        for i in range(bx):
-            c = i + SMOOTH
-            total = v[c] * WIDE[SMOOTH]
-            for t in range(1, SMOOTH + 1):
-                total = total + (v[c + t] + v[c - t]) * WIDE[SMOOTH + t]
-            smooth[f, i, ys, zz] = total
-        return carry
-
-    lax.fori_loop(0, 6 * tiles_y * tiles_z, smooth_x, 0)
-
-    def finish(i, carry):
-        s = right(
-            jnp.concatenate([smooth[f, i] for f in range(6)], axis=0), zs[:, :z], zs[:, z:])
-        jxx, jyy, jzz, jxy, jxz, jyz = (s[f * by:(f + 1) * by] for f in range(6))
-        trace = jxx + jyy + jzz
-        shift = 0.1 * trace + 1e-06
-        a, b, c = jxx + shift, jyy + shift, jzz + shift
-        cof = a * b - jxy * jxy
-        det = (
-            a * (b * c - jyz * jyz)
-            - jxy * (jxy * c - jyz * jxz)
-            + jxz * (jxy * jyz - b * jxz)
-        )
-        weight = trace * cof / det
-        label = phases[i]
-        base = jnp.where(label == 0, table[0, 0], jnp.where(label == 1, table[0, 1], table[0, 2]))
-        aniso = jnp.where(label == 0, table[1, 0], jnp.where(label == 1, table[1, 1], table[1, 2]))
-        cond[POT_X + i, POT_Y:POT_Y + by] = base + 0.1 * aniso * weight
-        return carry
-
-    for k, (low, high) in enumerate(bands):
-        lax.fori_loop(low, high, finish, 0)
-        if k == 1:
-            conds.start_x(0)
-            conds.start_y(0)
-        if k >= 1:
-            conds.start_y(k)
+
+    def finish(rows):
+        every = right(
+            jnp.concatenate([smooth[f, i] for i in rows for f in range(6)], axis=0),
+            zs[:, :z], zs[:, z:])
+        for n, i in enumerate(rows):
+            s = every[n * 6 * by:(n + 1) * 6 * by]
+            jxx, jyy, jzz, jxy, jxz, jyz = (s[f * by:(f + 1) * by] for f in range(6))
+            trace = jxx + jyy + jzz
+            shift = 0.1 * trace + 1e-06
+            a, b, c = jxx + shift, jyy + shift, jzz + shift
+            cof = a * b - jxy * jxy
+            det = (
+                a * (b * c - jyz * jyz)
+                - jxy * (jxy * c - jyz * jxz)
+                + jxz * (jxy * jyz - b * jxz)
+            )
+            weight = trace * cof / det
+            label = phases[i]
+            base = jnp.where(
+                label == 0, table[0, 0], jnp.where(label == 1, table[0, 1], table[0, 2]))
+            aniso = jnp.where(
+                label == 0, table[1, 0], jnp.where(label == 1, table[1, 1], table[1, 2]))
+            cond[POT_X + i, POT_Y:POT_Y + by] = base + 0.1 * aniso * weight
+
+    finish([i for low, high in bands[:2] for i in range(low, high)])
+    conds.start_x(0)
+    conds.start_y(0)
+    conds.start_y(1)
+    for k in range(2, len(bands)):
+        finish(list(range(*bands[k])))
+        conds.start_y(k)
     conds.forward(0)
 
     own_start.wait()
@@ -417,15 +435,22 @@
     return 2.0 * p * q / jnp.where(total > 0, total, 1.0)
 
 
-PAIR = 2
-
-
-def sweep_kernel(cond, start, centre, out, kx, y0, y1, z0, z1, inv, one, two, sem):
+def step_of(count):
+    return max(n for n in (1, 2, 3, 4) if count % n == 0)
+
+
+def sweep_kernel(cond_in, start_in, centre, out, cond, start, kx, y0, y1, z0, z1, inv, one, two,
+                 *sems):
     rows, wide, z = cond.shape
+    get_cond = pltpu.make_async_copy(cond_in, cond, sems[0])
+    get_start = pltpu.make_async_copy(start_in, start, sems[1])
+    get_cond.start()
+    get_start.start()
+    get_cond.wait()
     copy = pltpu.make_async_copy(
-        cond.at[pl.ds(POT_X, rows - 2 * POT_X), pl.ds(POT_Y, wide - 2 * POT_Y)], centre, sem)
+        cond.at[pl.ds(POT_X, rows - 2 * POT_X), pl.ds(POT_Y, wide - 2 * POT_Y)], centre, sems[2])
     copy.start()
-    lane = lax.broadcasted_iota(jnp.int32, (PAIR, wide, z), 2)
+    lane = lax.broadcasted_iota(jnp.int32, (1, wide, z), 2)
     at_low, at_high = lane == 0, lane == z - 1
 
     def roll_y(v, s):
@@ -435,53 +460,50 @@
         return pltpu.roll(v, s % z, 2)
 
     kx[0] = harmonic(cond[0], cond[1])
+    size = 2
 
     def coefficients(step, carry):
-        j = 1 + step * PAIR
-        c = cond[pl.ds(j, PAIR)]
-        x_up = harmonic(c, cond[pl.ds(j + 1, PAIR)])
+        j = 1 + step * size
+        c = cond[pl.ds(j, size)]
+        x_up = harmonic(c, cond[pl.ds(j + 1, size)])
         y_up = harmonic(c, roll_y(c, -1))
         z_up = harmonic(c, roll_z(c, -1))
-        x_down = jnp.concatenate([kx[j - 1][None], x_up[:PAIR - 1]], axis=0)
+        x_down = jnp.concatenate([kx[j - 1][None], x_up[:size - 1]], axis=0)
         y_down = roll_y(y_up, 1)
         low = jnp.where(at_low, c, roll_z(z_up, 1))
         high = jnp.where(at_high, c, z_up)
         total = x_down + x_up + y_down + y_up + low + high
-        kx[pl.ds(j, PAIR)] = x_up
-        y0[pl.ds(j, PAIR)] = y_down
-        y1[pl.ds(j, PAIR)] = y_up
-        z0[pl.ds(j, PAIR)] = low
-        z1[pl.ds(j, PAIR)] = high
-        inv[pl.ds(j, PAIR)] = 1.0 / jnp.where(total > 0, total, 1.0)
+        kx[pl.ds(j, size)] = x_up
+        y0[pl.ds(j, size)] = y_down
+        y1[pl.ds(j, size)] = y_up
+        z0[pl.ds(j, size)] = low
+        z1[pl.ds(j, size)] = high
+        inv[pl.ds(j, size)] = 1.0 / jnp.where(total > 0, total, 1.0)
         return carry
 
-    lax.fori_loop(0, (rows - 2) // PAIR, coefficients, 0)
-
-    def sweep(src, put, first, last):
+    lax.fori_loop(0, (rows - 2) // size, coefficients, 0)
+    get_start.wait()
+
+    def sweep(src, dst, shift, cols, first, last):
+        size = step_of(last - first)
+
         def step(k, carry):
-            j = first + k * PAIR
-            at = pl.ds(j, PAIR)
+            j = first + k * size
+            at = pl.ds(j, size)
             p = src[at]
-            numer = kx[pl.ds(j - 1, PAIR)] * src[pl.ds(j - 1, PAIR)]
-            numer = numer + kx[at] * src[pl.ds(j + 1, PAIR)]
+            numer = kx[pl.ds(j - 1, size)] * src[pl.ds(j - 1, size)]
+            numer = numer + kx[at] * src[pl.ds(j + 1, size)]
             numer = numer + y0[at] * roll_y(p, 1) + y1[at] * roll_y(p, -1)
             numer = numer + z0[at] * jnp.where(at_low, 1.0, roll_z(p, 1))
             numer = numer + z1[at] * jnp.where(at_high, 0.0, roll_z(p, -1))
-            put(j, numer * inv[at])
+            value = numer * inv[at]
+            dst[pl.ds(j - shift, size)] = value[:, cols:wide - cols]
             return carry
-        lax.fori_loop(0, (last - first) // PAIR, step, 0)
-
-    def into(ref):
-        def put(j, v):
-            ref[pl.ds(j, PAIR)] = v
-        return put
-
-    def put_out(j, v):
-        out[pl.ds(j - POT_X, PAIR)] = v[:, POT_Y:wide - POT_Y]
-
-    sweep(start, into(one), 1, rows - 1)
-    sweep(one, into(two), 2, rows - 2)
-    sweep(two, put_out, 3, rows - 3)
+        lax.fori_loop(0, (last - first) // size, step, 0)
+
+    sweep(start, one, 0, 0, 1, rows - 1)
+    sweep(one, two, 0, 0, 2, rows - 2)
+    sweep(two, out, POT_X, POT_Y, 3, rows - 3)
     copy.wait()
 
 
@@ -492,10 +514,10 @@
     return pl.pallas_call(
         sweep_kernel,
         out_shape=[brick, brick],
-        in_specs=[vmem, vmem],
-        out_specs=[pl.BlockSpec(memory_space=pltpu.HBM), vmem],
-        scratch_shapes=[pltpu.VMEM((rows, wide, z), F32)] * 8 + [pltpu.SemaphoreType.DMA],
-        compiler_params=pltpu.CompilerParams(vmem_limit_bytes=32 * 1024 * 1024),
+        in_specs=[pl.BlockSpec(memory_space=pl.ANY)] * 2,
+        out_specs=[pl.BlockSpec(memory_space=pl.ANY), vmem],
+        scratch_shapes=[pltpu.VMEM((rows, wide, z), F32)] * 10 + [pltpu.SemaphoreType.DMA] * 3,
+        compiler_params=pltpu.CompilerParams(vmem_limit_bytes=VMEM_LIMIT),
     )(cond_ext, pot_ext)
 
 

time: 51.6 us -> 49.4 us (0.957)
  local copies, waits for them, and re-layouts: 2.47 us -> 0 us
    unnamed x4 -> x0, local copies, waits for them, and re-layouts: 2.47 us -> none
    pallas_call x1, Pallas kernels: 6.2 us -> 6.73 us  [sweeps(): pl.pallas_call(sweep_kernel, out_shape=[brick, brick], in_specs=[pl.Block...]
where the time goes in v3:
time: 49.4 us; the launch traced here: 49.3 us
  Pallas kernels  48.6 us (98%)
  between operations  0.64 us (1%)
    pallas_call x1, Pallas kernels, tensor(): pl.pallas_call(tensor_kernel, out_shape=[outer, outer], in_specs=[anywher...  41.9 us
    pallas_call x1, Pallas kernels, sweeps(): pl.pallas_call(sweep_kernel, out_shape=[brick, brick], in_specs=[pl.Block...  6.73 us

profile of v3, /device:TPU:1, one launch (start us, length us, event | category | flops | bytes accessed | tf_op | source)
XLA Modules:
  0.0 49.3 jit_solution(9883959971952394782)
XLA Ops:
  0.6 41.9 %shard_map.95 = (f32[22,48,256]{2,1,0:T(8,128)}, f32[22,48,256]{2,1,0:T(8,128)}) custom-call(f32[16,32,256]{2,1,0:T(8,128)} %image.1, s32[16,32,256]{2,1,0:T(8,128)} %phases_in.1, f32[2,3]{1,0:T(2,128)} %table_in.1, f32[16,32,256]{2,1,0:T(8,128)} %start.1, bf16[128,192]{1,0:T(8,128)(2,1)} %constant.8.clone.wg_in, bf16[32,192]{1,0:T(8,128)(2,1)} %constant.9.clone.ws_in, ...), custom_call_target="tpu_custom_call" | custom-call | tf_op jit(solution)/shard_map/pallas_call | solution.py:414
  42.5 6.7 %shard_map.96 = (f32[16,32,256]{2,1,0:T(8,128)}, f32[16,32,256]{2,1,0:T(8,128)}) custom-call(f32[22,48,256]{2,1,0:T(8,128)} %get-tuple-element.4.cond_in, f32[22,48,256]{2,1,0:T(8,128)} %get-tuple-element.5.start_in), custom_call_target="tpu_custom_call" | custom-call | tf_op jit(solution)/shard_map/pallas_call | solution.py:514

commit v4 on v3

--- a/solution.py
+++ b/solution.py
@@ -303,11 +303,7 @@
     centre = rows_x // 2
     img.forward(0)
     img.wait_y(0)
-    img.forward(1)
     derive_both(centre - STEP, centre)
-    img.forward(2)
-    pots.start_x(0)
-    pots.start_y(0)
     tiles_y, tiles_z = by // 8, z // 128
 
     def smooth_x(known, ready, add):
@@ -335,8 +331,11 @@
 
     last = len(IMG_CUTS) - 1
     for c in range(last):
+        img.forward(c + 1)
         img.wait_corner(c)
         derive_both(centre - (c + 2) * STEP, centre + (c + 1) * STEP)
+    pots.start_x(0)
+    pots.start_y(0)
     inner = range(STEP, rows_x - STEP)
     smooth_x(inner, (), False)
     img.wait_corner(last)

time: 49.4 us -> 49.2 us (level); the launches traced: 49.3 us -> 48.4 us
  Pallas kernels: 48.6 us -> 47.8 us
    pallas_call x1, Pallas kernels: 41.9 us -> 41.1 us  [tensor(): pl.pallas_call(tensor_kernel, out_shape=[outer, outer], in_specs=[anywher...]
where the time goes in v4:
time: 49.2 us; the launch traced here: 48.4 us
  Pallas kernels  47.8 us (97%)
  between operations  0.64 us (1%)
    pallas_call x1, Pallas kernels, tensor(): pl.pallas_call(tensor_kernel, out_shape=[outer, outer], in_specs=[anywher...  41.1 us
    pallas_call x1, Pallas kernels, sweeps(): pl.pallas_call(sweep_kernel, out_shape=[brick, brick], in_specs=[pl.Block...  6.73 us

profile of v4, /device:TPU:1, one launch (start us, length us, event | category | flops | bytes accessed | tf_op | source)
XLA Modules:
  0.0 48.4 jit_solution(2461559531152494718)
XLA Ops:
  0.6 41.1 %shard_map.95 = (f32[22,48,256]{2,1,0:T(8,128)}, f32[22,48,256]{2,1,0:T(8,128)}) custom-call(f32[16,32,256]{2,1,0:T(8,128)} %image.1, s32[16,32,256]{2,1,0:T(8,128)} %phases_in.1, f32[2,3]{1,0:T(2,128)} %table_in.1, f32[16,32,256]{2,1,0:T(8,128)} %start.1, bf16[128,192]{1,0:T(8,128)(2,1)} %constant.8.clone.wg_in, bf16[32,192]{1,0:T(8,128)(2,1)} %constant.9.clone.ws_in, ...), custom_call_target="tpu_custom_call" | custom-call | tf_op jit(solution)/shard_map/pallas_call | solution.py:413
  41.7 6.7 %shard_map.96 = (f32[16,32,256]{2,1,0:T(8,128)}, f32[16,32,256]{2,1,0:T(8,128)}) custom-call(f32[22,48,256]{2,1,0:T(8,128)} %get-tuple-element.4.cond_in, f32[22,48,256]{2,1,0:T(8,128)} %get-tuple-element.5.start_in), custom_call_target="tpu_custom_call" | custom-call | tf_op jit(solution)/shard_map/pallas_call | solution.py:513
